TPU v7x, 256 devices: a whole 4x4x8 slice. The times are simulated.
256 devices in a mesh: tm: 32 (over y, z_hi, core), height: 4 (over x), head: 2 (over z_lo).
Axes of the slice: x: 4, y: 4, z: 8 (z_hi: 4, z_lo: 2; z = z_hi * 2 + z_lo), core: 2. Of those that a mesh axis runs over, the one named last changes fastest.
Arguments:
- queries: bfloat16 [65536, 1536], P(('tm', 'height'), 'head'), may hold values from -5 to 5
- keys: bfloat16 [65536, 1536], P(('tm', 'height'), 'head'), may hold values from -5 to 5
- values: bfloat16 [65536, 1536], P(('tm', 'height'), 'head'), may hold values from -6 to 6
- out_weight: bfloat16 [1536, 3072], P('head'), may hold values from -0.15625 to 0.15625
- kv_list: int32 [128, 8], P(('tm', 'height')), may hold values from 0 to 127, as said below
- kv_count: int32 [128], P(('tm', 'height')), may hold values from 1 to 8, as said below
Outputs:
- mixed: bfloat16 [65536, 3072], P(('tm', 'height'), 'head')
Inputs may be any that keep to these rules, and one draw needn't show every extreme that they name: Entries of kv_list[b] at positions below kv_count[b] are distinct; the first is b; each other is one frame away in the same band (b + 4 or b - 4), one band away in the same frame (b + 1 or b - 1 within the frame), or in the same band at a frame distance that is a power of two from 2 to below 32. Entries at later positions equal b. `kv_count`: number of listed key blocks; some block has 8.
All inputs are finite; a program needn't handle non-finite values.
Results may differ from a plain program's by a relative error of at most 0.015.
Values may be sent and summed in bfloat16 or wider, within the bound.
A program may use at most 192 MiB of HBM per device.

v0:
```python
import jax
import jax.numpy as jnp
from jax import lax
from jax.sharding import PartitionSpec as P

HEAD_DIM = 128


def extended(block, sides, width):
    for axis, dim in sides:
        count = lax.axis_size(axis)
        forward = [(i, i + 1) for i in range(count - 1)]
        backward = [(target, source) for source, target in forward]
        low = lax.ppermute(
            lax.slice_in_dim(block, block.shape[dim] - width, None, axis=dim), axis, forward
        )
        high = lax.ppermute(lax.slice_in_dim(block, 0, width, axis=dim), axis, backward)
        block = jnp.concatenate([low, block, high], axis=dim)
    return block


def passed_along(value, axis, steps):
    count = lax.axis_size(axis)
    initial, last = (max(0, -steps), min(count, count - steps))
    return lax.ppermute(value, axis, [(source, source + steps) for source in range(initial, last)])


def body(queries, keys, values, out_weight, kv_list, kv_count):
    tokens_here = queries.shape[0]
    feature_width = queries.shape[1]
    head_count = feature_width // HEAD_DIM
    score_scale = HEAD_DIM ** (-0.5)
    frames = lax.axis_size("tm")
    band_count = lax.axis_size("height")
    frame_at = lax.axis_index("tm")
    band_at = lax.axis_index("height")
    paired = jnp.stack([keys, values])
    distances = []
    distance = 2
    while distance < frames:
        distances.append(distance)
        distance = distance * 2
    beside_all = extended(paired[None, None], (("tm", 0), ("height", 1)), 1)
    nearby = [
        beside_all[1, 1],
        beside_all[0, 1],
        beside_all[2, 1],
        beside_all[1, 0],
        beside_all[1, 2],
    ]
    distant = []
    for distance in distances:
        for direction in (-1, 1):
            distant.append(passed_along(paired, "tm", direction * distance))
    candidates = jnp.stack(nearby + distant)
    listed = kv_list[0]
    listed_count = kv_count[0]
    frame_offset = listed // band_count - frame_at
    band_offset = listed % band_count - band_at
    slots_of = jnp.zeros_like(listed)
    slots_of = jnp.where(frame_offset == -1, 1, slots_of)
    slots_of = jnp.where(frame_offset == 1, 2, slots_of)
    slots_of = jnp.where(band_offset == -1, 3, slots_of)
    slots_of = jnp.where(band_offset == 1, 4, slots_of)
    for position, distance in enumerate(distances):
        slots_of = jnp.where(frame_offset == distance, 5 + 2 * position, slots_of)
        slots_of = jnp.where(frame_offset == -distance, 6 + 2 * position, slots_of)
    query_rows = queries.reshape(tokens_here, head_count, HEAD_DIM)

    def attend_block(turn, carry):
        largest, totals, weighted = carry
        chosen_pair = lax.dynamic_index_in_dim(candidates, slots_of[turn], 0, keepdims=False)
        key_rows = chosen_pair[0].reshape(tokens_here, head_count, HEAD_DIM)
        value_rows = chosen_pair[1].reshape(tokens_here, head_count, HEAD_DIM)
        scores = (
            jnp.einsum("qhd,khd->hqk", query_rows, key_rows, preferred_element_type=jnp.float32)
            * score_scale
        )
        new_largest = jnp.maximum(largest, jnp.max(scores, axis=-1))
        rescale = jnp.exp(largest - new_largest)
        weights = jnp.exp(scores - new_largest[:, :, None])
        totals = totals * rescale + jnp.sum(weights, axis=-1)
        update = jnp.einsum(
            "hqk,khd->qhd",
            weights.astype(jnp.bfloat16),
            value_rows,
            preferred_element_type=jnp.float32,
        )
        weighted = weighted * jnp.transpose(rescale)[:, :, None] + update
        return (new_largest, totals, weighted)

    start_largest = jnp.full((head_count, tokens_here), -1e30, jnp.float32)
    start_totals = jnp.zeros((head_count, tokens_here), jnp.float32)
    start_weighted = jnp.zeros((tokens_here, head_count, HEAD_DIM), jnp.float32)
    largest, totals, weighted = lax.fori_loop(
        0, listed_count, attend_block, (start_largest, start_totals, start_weighted)
    )
    attended = (
        (weighted / jnp.transpose(totals)[:, :, None])
        .astype(jnp.bfloat16)
        .reshape(tokens_here, feature_width)
    )
    partial_value = jnp.dot(attended, out_weight, preferred_element_type=jnp.float32)
    mixed_out = lax.psum_scatter(
        partial_value.astype(jnp.bfloat16), "head", scatter_dimension=1, tiled=True
    )
    return mixed_out


def solution(mesh):
    return jax.shard_map(
        body,
        mesh=mesh,
        in_specs=(
            P(("tm", "height"), "head"),
            P(("tm", "height"), "head"),
            P(("tm", "height"), "head"),
            P("head", None),
            P(("tm", "height"), None),
            P(("tm", "height")),
        ),
        out_specs=P(("tm", "height"), "head"),
        check_vma=False,
    )
```

profile of v0, /device:TPU:44, one launch (start us, length us, event | category | flops | bytes accessed | tf_op | source)
XLA Modules:
  0.0 474.3 jit_solution(15379622907626728863)
XLA Ops:
  10.7 2.0 collective-permute-start
  12.8 6.7 %collective-permute-start.1 = (bf16[1,1,2,512,768]{3,4,2,1,0:T(8,128)(2,1)S(1)}, bf16[1,1,2,512,768]{3,4,2,1,0:T(8,128)(2,1)S(1)}, u32[]{:S(2)}, u32[]{:S(2)}) collective-permute-start(bf16[1,1,2,512,768]{3,4,2,1,0:T(8,128)(2,1)S(1)} %get-tuple-element.82), channel_id=1, source_target_pairs={{8,0},{16,8},{24,16},{32,24},{40,32},{48,40},{56,48},{64,56},{72,6... | collective-permute-start | bytes 4718600 | tf_op jit(solution)/shard_map/ppermute | solution.py:17
  19.4 33.0 %collective-permute-done = bf16[1,1,2,512,768]{3,4,2,1,0:T(8,128)(2,1)S(1)} collective-permute-done((bf16[1,1,2,512,768]{3,4,2,1,0:T(8,128)(2,1)S(1)}, bf16[1,1,2,512,768]{3,4,2,1,0:T(8,128)(2,1)S(1)}, u32[]{:S(2)}, u32[]{:S(2)}) %collective-permute-start) | collective-permute-done | bytes 1572896 | tf_op jit(solution)/shard_map/ppermute | solution.py:14
  52.4 2.6 pad_maximum_fusion
  55.5 3.1 collective-permute-start.2
  58.6 2.7 collective-permute-start.3
  61.4 4.7 %collective-permute-start.4 = (bf16[2,512,768]{1,2,0:T(8,128)(2,1)}, bf16[2,512,768]{1,2,0:T(8,128)(2,1)}, u32[]{:S(2)}, u32[]{:S(2)}) collective-permute-start(bf16[2,512,768]{1,2,0:T(8,128)(2,1)} %get-tuple-element.81), channel_id=1, source_target_pairs={{16,0},{24,8},{32,16},{40,24},{48,32},{56,40},{64,48},{72,56},{80,... | collective-permute-start | bytes 4718600 | tf_op jit(solution)/shard_map/ppermute | solution.py:25
  66.1 2.0 collective-permute-start.5
  68.1 5.5 %collective-permute-start.6 = (bf16[2,512,768]{1,2,0:T(8,128)(2,1)}, bf16[2,512,768]{1,2,0:T(8,128)(2,1)}, u32[]{:S(2)}, u32[]{:S(2)}) collective-permute-start(bf16[2,512,768]{1,2,0:T(8,128)(2,1)} %get-tuple-element.81), channel_id=1, source_target_pairs={{32,0},{40,8},{48,16},{56,24},{64,32},{72,40},{80,48},{88,56},{96,... | collective-permute-start | bytes 4718600 | tf_op jit(solution)/shard_map/ppermute | solution.py:25
  75.0 1.5 copy.14
  76.9 2.6 bitcast_dynamic-update-slice_fusion.9
  79.5 22.9 %collective-permute-done.4 = bf16[2,512,768]{1,2,0:T(8,128)(2,1)} collective-permute-done((bf16[2,512,768]{1,2,0:T(8,128)(2,1)}, bf16[2,512,768]{1,2,0:T(8,128)(2,1)}, u32[]{:S(2)}, u32[]{:S(2)}) %collective-permute-start.4) | collective-permute-done | bytes 1572896 | tf_op jit(solution)/shard_map/ppermute | solution.py:25
  102.4 7.6 %collective-permute-start.7 = (bf16[2,512,768]{1,2,0:T(8,128)(2,1)}, bf16[2,512,768]{1,2,0:T(8,128)(2,1)S(1)}, u32[]{:S(2)}, u32[]{:S(2)}) collective-permute-start(bf16[2,512,768]{1,2,0:T(8,128)(2,1)} %get-tuple-element.81), channel_id=1, source_target_pairs={{0,32},{8,40},{16,48},{24,56},{32,64},{40,72},{48,80},{56,88},{64,... | collective-permute-start | bytes 4718600 | tf_op jit(solution)/shard_map/ppermute | solution.py:25
  111.2 47.8 %collective-permute-done.2 = bf16[3,1,2,512,768]{3,4,2,1,0:T(8,128)(2,1)} collective-permute-done((bf16[3,1,2,512,768]{3,4,2,1,0:T(8,128)(2,1)}, bf16[3,1,2,512,768]{3,4,2,1,0:T(8,128)(2,1)}, u32[]{:S(2)}, u32[]{:S(2)}) %collective-permute-start.2) | collective-permute-done | bytes 4718624 | tf_op jit(solution)/shard_map/ppermute | solution.py:14
  159.0 1.9 collective-permute-start.8
  160.9 2.7 fusion.12
  163.6 3.9 collective-permute-start.9
  167.5 2.7 fusion.11
  171.5 2.8 bitcast_dynamic-update-slice_fusion.7
  174.2 66.4 %collective-permute-start.11 = (bf16[2,512,768]{1,2,0:T(8,128)(2,1)}, bf16[2,512,768]{1,2,0:T(8,128)(2,1)S(1)}, u32[]{:S(2)}, u32[]{:S(2)}) collective-permute-start(bf16[2,512,768]{1,2,0:T(8,128)(2,1)} %get-tuple-element.81), channel_id=1, source_target_pairs={{0,128},{8,136},{16,144},{24,152},{32,160},{40,168},{48,176},{56,1... | collective-permute-start | bytes 4718600 | tf_op jit(solution)/shard_map/ppermute | solution.py:25
  240.7 2.7 bitcast_dynamic-update-slice_fusion.6
  243.3 2.7 bitcast_dynamic-update-slice_fusion.5
  246.0 21.2 %collective-permute-done.7 = bf16[2,512,768]{1,2,0:T(8,128)(2,1)S(1)} collective-permute-done((bf16[2,512,768]{1,2,0:T(8,128)(2,1)}, bf16[2,512,768]{1,2,0:T(8,128)(2,1)S(1)}, u32[]{:S(2)}, u32[]{:S(2)}) %collective-permute-start.7) | collective-permute-done | bytes 1572896 | tf_op jit(solution)/shard_map/ppermute | solution.py:25
  273.7 51.6 %while.14 = (s32[]{:T(128)}, f32[6,512]{1,0:T(8,128)S(1)}, f32[6,512]{1,0:T(8,128)S(1)}, f32[512,6,128]{0,2,1:T(8,128)S(1)}, s32[]{:T(128)}, /*index=5*/s32[8]{0...) while((s32[]{:T(128)}, f32[6,512]{1,0:T(8,128)S(1)}, ...), condition=%wide.region_3.4_spmd, body=%wide.region_0.3_spmd.sunk | while | flops 818684928 | bytes 27721960 | solution.py:95
  280.6 1.7 bitcast_add_fusion.2
  289.0 1.7 bitcast_add_fusion.2
  297.5 1.7 bitcast_add_fusion.2
  306.0 1.7 bitcast_add_fusion.2
  314.5 1.7 bitcast_add_fusion.2
  323.0 1.7 bitcast_add_fusion.2
  325.6 6.4 %convolution_convert_fusion = bf16[512,3072]{1,0:T(8,128)(2,1)} fusion(bf16[512,768]{0,1:T(8,128)(2,1)S(1)} %bitcast.105, bf16[768,3072]{1,0:T(8,128)(2,1)} %param.11), kind=kOutput, calls=%fused_computation.16 | convolution fusion | flops 2417491968 | bytes 8650752 | tf_op jit(solution)/shard_map/dot_general | solution.py:103
  332.0 135.5 %reduce-scatter.2.cloned.1.call-done = bf16[512,1536]{1,0:T(8,128)(2,1)} async-done(((bf16[512,3072]{1,0:T(8,128)(2,1)}), bf16[512,1536]{1,0:T(8,128)(2,1)}) %reduce-scatter.2.cloned.1.call-update) | async-done | bytes 1572880 | tf_op jit(solution)/shard_map/reduce_scatter | solution.py:104
  (77 shorter events, 40.7 us)
Async XLA Ops:
  6.5 460.9 %reduce-scatter.2.cloned.1.call-start = ((), (), s32[]{:S(2)}) async-start(), calls=%async_computation.1 | async-start | bytes 4718592 | tf_op jit(solution)/shard_map/reduce_scatter | solution.py:104
  10.7 62.9 %copy-start.3 = (s32[1,8]{1,0:T(1,128)S(1)}, s32[1,8]{1,0:T(1,128)}, u32[]{:S(2)}) copy-start(s32[1,8]{1,0:T(1,128)} %param.12) | copy-start | bytes 100
  10.7 41.7 %collective-permute-start = (bf16[1,1,2,512,768]{3,4,2,1,0:T(8,128)(2,1)S(1)}, bf16[1,1,2,512,768]{3,4,2,1,0:T(8,128)(2,1)S(1)}, u32[]{:S(2)}, u32[]{:S(2)}) collective-permute-start(bf16[1,1,2,512,768]{3,4,2,1,0:T(8,128)(2,1)S(1)} %get-tuple-element.82), channel_id=1, source_target_pairs={{0,8},{8,16},{16,24},{24,32},{32,40},{40,48},{48,56},{56,64},{64,7... | collective-permute-start | bytes 4718600 | tf_op jit(solution)/shard_map/ppermute | solution.py:14
  12.8 39.7 %collective-permute-start.1 = (bf16[1,1,2,512,768]{3,4,2,1,0:T(8,128)(2,1)S(1)}, bf16[1,1,2,512,768]{3,4,2,1,0:T(8,128)(2,1)S(1)}, u32[]{:S(2)}, u32[]{:S(2)}) collective-permute-start(bf16[1,1,2,512,768]{3,4,2,1,0:T(8,128)(2,1)S(1)} %get-tuple-element.82), channel_id=1, source_target_pairs={{8,0},{16,8},{24,16},{32,24},{40,32},{48,40},{56,48},{64,56},{72,6... | collective-permute-start | bytes 4718600 | tf_op jit(solution)/shard_map/ppermute | solution.py:17
  52.4 2.6 copy-start.2
  52.4 3.1 copy-start
  55.5 103.5 %collective-permute-start.2 = (bf16[3,1,2,512,768]{3,4,2,1,0:T(8,128)(2,1)}, bf16[3,1,2,512,768]{3,4,2,1,0:T(8,128)(2,1)}, u32[]{:S(2)}, u32[]{:S(2)}) collective-permute-start(bf16[3,1,2,512,768]{3,4,2,1,0:T(8,128)(2,1)} %pad_maximum_fusion), channel_id=1, source_target_pairs={{0,2},{2,4},{4,6},{1,3},{3,5},{5,7},{8,10},{10,12},{12,14},{9,11},... | collective-permute-start | bytes 14155784 | tf_op jit(solution)/shard_map/ppermute | solution.py:14
  58.6 105.0 %collective-permute-start.3 = (bf16[3,1,2,512,768]{3,4,2,1,0:T(8,128)(2,1)}, bf16[3,1,2,512,768]{3,4,2,1,0:T(8,128)(2,1)}, u32[]{:S(2)}, u32[]{:S(2)}) collective-permute-start(bf16[3,1,2,512,768]{3,4,2,1,0:T(8,128)(2,1)} %pad_maximum_fusion), channel_id=1, source_target_pairs={{2,0},{4,2},{6,4},{3,1},{5,3},{7,5},{10,8},{12,10},{14,12},{11,9},... | collective-permute-start | bytes 14155784 | tf_op jit(solution)/shard_map/ppermute | solution.py:17
  61.4 41.0 %collective-permute-start.4 = (bf16[2,512,768]{1,2,0:T(8,128)(2,1)}, bf16[2,512,768]{1,2,0:T(8,128)(2,1)}, u32[]{:S(2)}, u32[]{:S(2)}) collective-permute-start(bf16[2,512,768]{1,2,0:T(8,128)(2,1)} %get-tuple-element.81), channel_id=1, source_target_pairs={{16,0},{24,8},{32,16},{40,24},{48,32},{56,40},{64,48},{72,56},{80,... | collective-permute-start | bytes 4718600 | tf_op jit(solution)/shard_map/ppermute | solution.py:25
  66.1 104.1 %collective-permute-start.5 = (bf16[2,512,768]{1,2,0:T(8,128)(2,1)}, bf16[2,512,768]{1,2,0:T(8,128)(2,1)}, u32[]{:S(2)}, u32[]{:S(2)}) collective-permute-start(bf16[2,512,768]{1,2,0:T(8,128)(2,1)} %get-tuple-element.81), channel_id=1, source_target_pairs={{0,16},{8,24},{16,32},{24,40},{32,48},{40,56},{48,64},{56,72},{64,... | collective-permute-start | bytes 4718600 | tf_op jit(solution)/shard_map/ppermute | solution.py:25
  68.1 106.1 %collective-permute-start.6 = (bf16[2,512,768]{1,2,0:T(8,128)(2,1)}, bf16[2,512,768]{1,2,0:T(8,128)(2,1)}, u32[]{:S(2)}, u32[]{:S(2)}) collective-permute-start(bf16[2,512,768]{1,2,0:T(8,128)(2,1)} %get-tuple-element.81), channel_id=1, source_target_pairs={{32,0},{40,8},{48,16},{56,24},{64,32},{72,40},{80,48},{88,56},{96,... | collective-permute-start | bytes 4718600 | tf_op jit(solution)/shard_map/ppermute | solution.py:25
  75.0 35.0 %copy-start.1 = (bf16[1,1,2,512,768]{3,4,2,1,0:T(8,128)(2,1)S(1)}, bf16[1,1,2,512,768]{3,4,2,1,0:T(8,128)(2,1)}, u32[]{:S(2)}) copy-start(bf16[1,1,2,512,768]{3,4,2,1,0:T(8,128)(2,1)} %copy-done) | copy-start | bytes 4718596
  102.4 164.8 %collective-permute-start.7 = (bf16[2,512,768]{1,2,0:T(8,128)(2,1)}, bf16[2,512,768]{1,2,0:T(8,128)(2,1)S(1)}, u32[]{:S(2)}, u32[]{:S(2)}) collective-permute-start(bf16[2,512,768]{1,2,0:T(8,128)(2,1)} %get-tuple-element.81), channel_id=1, source_target_pairs={{0,32},{8,40},{16,48},{24,56},{32,64},{40,72},{48,80},{56,88},{64,... | collective-permute-start | bytes 4718600 | tf_op jit(solution)/shard_map/ppermute | solution.py:25
  159.0 109.5 %collective-permute-start.8 = (bf16[2,512,768]{1,2,0:T(8,128)(2,1)}, bf16[2,512,768]{1,2,0:T(8,128)(2,1)S(1)}, u32[]{:S(2)}, u32[]{:S(2)}) collective-permute-start(bf16[2,512,768]{1,2,0:T(8,128)(2,1)} %get-tuple-element.81), channel_id=1, source_target_pairs={{64,0},{72,8},{80,16},{88,24},{96,32},{104,40},{112,48},{120,56},{... | collective-permute-start | bytes 4718600 | tf_op jit(solution)/shard_map/ppermute | solution.py:25
  163.6 106.1 %collective-permute-start.9 = (bf16[2,512,768]{1,2,0:T(8,128)(2,1)}, bf16[2,512,768]{1,2,0:T(8,128)(2,1)S(1)}, u32[]{:S(2)}, u32[]{:S(2)}) collective-permute-start(bf16[2,512,768]{1,2,0:T(8,128)(2,1)} %get-tuple-element.81), channel_id=1, source_target_pairs={{0,64},{8,72},{16,80},{24,88},{32,96},{40,104},{48,112},{56,120},{... | collective-permute-start | bytes 4718600 | tf_op jit(solution)/shard_map/ppermute | solution.py:25
  170.2 100.8 %collective-permute-start.10 = (bf16[2,512,768]{1,2,0:T(8,128)(2,1)}, bf16[2,512,768]{1,2,0:T(8,128)(2,1)S(1)}, u32[]{:S(2)}, u32[]{:S(2)}) collective-permute-start(bf16[2,512,768]{1,2,0:T(8,128)(2,1)} %get-tuple-element.81), channel_id=1, source_target_pairs={{128,0},{136,8},{144,16},{152,24},{160,32},{168,40},{176,48},{184,... | collective-permute-start | bytes 4718600 | tf_op jit(solution)/shard_map/ppermute | solution.py:25
  174.2 98.0 %collective-permute-start.11 = (bf16[2,512,768]{1,2,0:T(8,128)(2,1)}, bf16[2,512,768]{1,2,0:T(8,128)(2,1)S(1)}, u32[]{:S(2)}, u32[]{:S(2)}) collective-permute-start(bf16[2,512,768]{1,2,0:T(8,128)(2,1)} %get-tuple-element.81), channel_id=1, source_target_pairs={{0,128},{8,136},{16,144},{24,152},{32,160},{40,168},{48,176},{56,1... | collective-permute-start | bytes 4718600 | tf_op jit(solution)/shard_map/ppermute | solution.py:25
Sparse Core Ops, SparseCore 0:
  332.1 135.3 reduce-scatter.1
where the time goes:
time: 478 us; the launch traced here: 474 us
  waiting for transfers between devices  260 us (54%)
  starting transfers between devices  108 us (23%)
  local copies, waits for them, and re-layouts  41.5 us (9%)
  matrix products  22.6 us (5%)
  loops' own time  16.6 us (3%)
  between operations  13.6 us (3%)
  other arithmetic  11.8 us (2%)
    reduce_scatter x1, waiting for transfers between devices, body(): lax.psum_scatter(partial_value.astype(jnp.bfloat16), 'head', scatter_dime...  135 us
    ppermute x8, starting transfers between devices, passed_along(): lax.ppermute(value, axis, [(source, source + steps) for source in range(i...  93.3 us
    ppermute x2, waiting for transfers between devices, extended(): lax.ppermute(lax.slice_in_dim(block, block.shape[dim] - width, None, axis...  80.8 us
    ppermute x8, waiting for transfers between devices, passed_along(): lax.ppermute(value, axis, [(source, source + steps) for source in range(i...  44.1 us
    unnamed x22, local copies, waits for them, and re-layouts  27.3 us
    another operation x1, loops' own time, body(): lax.fori_loop(0, listed_count, attend_block, (start_largest, start_totals...  16.6 us
    dot_general x6, matrix products, attend_block(): jnp.einsum('hqk,khd->qhd', weights.astype(jnp.bfloat16), value_rows, pref...  10 us
  transfers between devices with their start and end apart: 13, of which 5 were waited for; matrix products, arithmetic and copies ran while one was open for 5% of the time, Pallas kernels for 0%

commit v1 on v0

v1 whole, which is shorter than its diff:
```python
import functools

import jax
import jax.numpy as jnp
from jax import lax
from jax.experimental import pallas as pl
from jax.experimental.pallas import tpu as pltpu
from jax.sharding import PartitionSpec as P

HEAD_DIM = 128
SIDE = 4
SCORE_SCALE = HEAD_DIM ** (-0.5) * 1.4426950408889634
UNLISTED = -1e30
ROWS = 128
AHEAD = 2

OWN, OTHER, XLO, XHI, YLO, YHI, ZHI, ZLO, ZOP, EDGE1, YOP, NEAR, EDGE2 = range(13)
SLOTS = 13

(TO_ZUP, TO_ZDOWN, RELAY_ZUP, RELAY_ZDOWN, TO_YDOWN, RELAY_YDOWN, TO_YUP, TO_EDGE1,
 TO_EDGE2, TO_XDOWN, TO_XUP, TO_CORE, TO_NEAR, TO_HEAD) = range(14)
SENDS = 14


def kernel(heads, kv_list, kv_count, q_ref, k_hbm, v_hbm, w_hbm, out_ref,
           kv, att, wbuf, total, top, sums, acc,
           send, recv, recv_v, att_recv, load, wload, wsend, wrecv):
    tm = lax.axis_index("tm")
    x = lax.axis_index("height")
    part = lax.axis_index("head")
    core = lax.rem(tm, 2)
    chip = lax.div(tm, 2)
    z = lax.rem(chip, SIDE)
    y = lax.div(chip, SIDE)
    far = lax.div(z, 2)
    sign = 1 - 2 * far
    ym = y * (1 - far) + (SIDE - 1 - y) * far
    zm = z * (1 - far) + (SIDE - 1 - z) * far

    def at(yy, zz, cc):
        return (yy * SIDE + zz) * 2 + cc

    zup, zdown = lax.rem(z + 1, SIDE), lax.rem(z + 3, SIDE)
    yup, ydown = lax.rem(y + sign + SIDE, SIDE), lax.rem(y - sign + SIDE, SIDE)
    dev_zup = (at(y, zup, core), x, part)
    dev_zdown = (at(y, zdown, core), x, part)
    dev_yup = (at(yup, z, core), x, part)
    dev_ydown = (at(ydown, z, core), x, part)
    dev_core = (at(y, z, 1 - core), x, part)
    dev_head = (tm, x, 1 - part)
    dev_x = [None] + [(tm, lax.rem(x + k, SIDE), part) for k in (1, 2, 3)]

    barrier = pltpu.get_barrier_semaphore()
    friends = [dev_zup, dev_zdown, dev_yup, dev_ydown, dev_core, dev_head] + dev_x[1:]
    for friend in friends:
        pl.semaphore_signal(barrier, inc=1, device_id=friend, device_id_type=pl.DeviceIdType.MESH)

    def loads(h):
        columns = pl.ds(pl.multiple_of(h * HEAD_DIM, HEAD_DIM), HEAD_DIM)
        return (pltpu.make_async_copy(k_hbm.at[:, columns], kv.at[OWN, h, 0], load.at[h, 0]),
                pltpu.make_async_copy(v_hbm.at[:, columns], kv.at[OWN, h, 1], load.at[h, 1]))

    for h in range(heads):
        for copy in loads(h):
            copy.start()
    width = w_hbm.shape[2] // 2
    mine = pl.ds(pl.multiple_of(part * width, HEAD_DIM), width)
    load_w = pltpu.make_async_copy(w_hbm.at[:, :, mine], wbuf.at[:, pl.ds(0, HEAD_DIM), :], wload)
    load_w.start()

    has_yup = ym < SIDE - 1
    has_ydown = ym > 0
    edge1_out = (zm == 0) & has_yup
    edge1_in = (zm == 0) & has_ydown
    has_near = ((core == 0) & (chip > 0)) | ((core == 1) & (chip < SIDE * SIDE - 1))
    gives_near = ((core == 1) & (chip > 0)) | ((core == 0) & (chip < SIDE * SIDE - 1))
    near_at_edge = ((core == 1) & (z == 0)) | ((core == 0) & (z == SIDE - 1))
    near_slot = ZHI + core * (ZLO - ZHI)
    edge_slot = ZLO * (1 - far) + ZHI * far

    def remote(kind, h, src, dst, sem, device):
        return pltpu.make_async_remote_copy(
            src_ref=src, dst_ref=dst, send_sem=send.at[kind, h], recv_sem=sem,
            device_id=device, device_id_type=pl.DeviceIdType.MESH)

    def pair(kind, h, source, slot, device):
        return remote(kind, h, kv.at[source, h], kv.at[slot, h], recv.at[slot, h], device)

    def arrival(slot, h, device=None):
        return pair(TO_CORE, h, slot, slot, dev_core)

    def copies(kind, h):
        if kind == TO_ZUP:
            return pair(kind, h, OWN, ZLO, dev_zup)
        if kind == TO_ZDOWN:
            return pair(kind, h, OWN, ZHI, dev_zdown)
        if kind == RELAY_ZUP:
            return remote(kind, h, kv.at[ZLO, h, 0], kv.at[ZOP, h, 0], recv.at[ZOP, h], dev_zup)
        if kind == RELAY_ZDOWN:
            return remote(kind, h, kv.at[ZHI, h, 1], kv.at[ZOP, h, 1], recv_v.at[h], dev_zdown)
        if kind == TO_YDOWN:
            return pair(kind, h, OWN, YHI, dev_ydown)
        if kind == RELAY_YDOWN:
            return pair(kind, h, YHI, YOP, dev_ydown)
        if kind == TO_YUP:
            return pair(kind, h, OWN, YLO, dev_yup)
        if kind == TO_EDGE1:
            return pair(kind, h, edge_slot, EDGE1, dev_yup)
        if kind == TO_EDGE2:
            return pair(kind, h, ZOP, EDGE2, dev_yup)
        if kind == TO_XDOWN:
            return pair(kind, h, OWN, XHI, dev_x[3])
        if kind == TO_XUP:
            return pair(kind, h, OWN, XLO, dev_x[1])
        if kind == TO_CORE:
            return pair(kind, h, OWN, OTHER, dev_core)
        if kind == TO_HEAD:
            return remote(kind, h, att.at[h, :, pl.ds(0, HEAD_DIM)],
                          att.at[h, :, pl.ds(HEAD_DIM, HEAD_DIM)], att_recv.at[h], dev_head)

    def near_copy(h, source):
        return pair(TO_NEAR, h, source, NEAR, dev_core)

    def send_own(h):
        for copy in loads(h):
            copy.wait()
        for kind in (TO_ZUP, TO_ZDOWN, TO_YDOWN):
            copies(kind, h).start()

        @pl.when(has_yup)
        def _():
            copies(TO_YUP, h).start()

        @pl.when(x > 0)
        def _():
            copies(TO_XDOWN, h).start()

        @pl.when(x < SIDE - 1)
        def _():
            copies(TO_XUP, h).start()

        copies(TO_CORE, h).start()

    def relay(h):
        arrival(ZLO, h).wait_recv()
        copies(RELAY_ZUP, h).start()
        arrival(ZHI, h).wait_recv()
        copies(RELAY_ZDOWN, h).start()

        @pl.when(edge1_out)
        def _():
            copies(TO_EDGE1, h).start()

        @pl.when(gives_near & jnp.logical_not(near_at_edge))
        def _():
            near_copy(h, near_slot).start()

        arrival(YHI, h).wait_recv()
        copies(RELAY_YDOWN, h).start()

    def relay_again(h):
        copies(RELAY_ZUP, h).wait_recv()
        copies(RELAY_ZDOWN, h).wait_recv()

        @pl.when(has_yup)
        def _():
            copies(TO_EDGE2, h).start()

        @pl.when(edge1_in)
        def _():
            arrival(EDGE1, h).wait_recv()

        @pl.when(gives_near & near_at_edge)
        def _():
            near_copy(h, EDGE1).start()

    group = heads // 2
    chunk = width // SIDE

    def weight_piece(device, sem, column0):
        return pltpu.make_async_remote_copy(
            src_ref=w_hbm.at[pl.ds(core * group, group), :,
                             pl.ds(pl.multiple_of(column0 + x * chunk, HEAD_DIM), chunk)],
            dst_ref=wbuf.at[pl.ds(core * group, group), pl.ds(HEAD_DIM, HEAD_DIM),
                            pl.ds(pl.multiple_of(x * chunk, HEAD_DIM), chunk)],
            send_sem=wsend.at[sem], recv_sem=wrecv.at[sem],
            device_id=device, device_id_type=pl.DeviceIdType.MESH)

    def weight_relay(k):
        piece = wbuf.at[pl.ds(core * group, group), pl.ds(HEAD_DIM, HEAD_DIM),
                        pl.ds(pl.multiple_of(x * chunk, HEAD_DIM), chunk)]
        return pltpu.make_async_remote_copy(
            src_ref=piece, dst_ref=piece, send_sem=wsend.at[k], recv_sem=wrecv.at[k],
            device_id=dev_x[k], device_id_type=pl.DeviceIdType.MESH)

    def weight_cross():
        piece = wbuf.at[pl.ds(core * group, group), pl.ds(HEAD_DIM, HEAD_DIM), :]
        return pltpu.make_async_remote_copy(
            src_ref=piece, dst_ref=piece, send_sem=wsend.at[SIDE], recv_sem=wrecv.at[SIDE],
            device_id=dev_core, device_id_type=pl.DeviceIdType.MESH)

    frame = tm
    bands = SIDE
    valid = [1 + 0 * z, 1 + 0 * z, x > 0, x < SIDE - 1, has_ydown, has_yup, z < SIDE - 1, z > 0,
             1 + 0 * z, edge1_in, 1 + 0 * z, has_near, has_ydown]
    valid = [jnp.int32(v) if isinstance(v, int) else v.astype(jnp.int32) for v in valid]
    block_of = [
        frame * bands + x,
        (frame + 1 - 2 * core) * bands + x,
        frame * bands + x - 1,
        frame * bands + x + 1,
        (frame - 8 * sign) * bands + x,
        (frame + 8 * sign) * bands + x,
        (frame + 2) * bands + x,
        (frame - 2) * bands + x,
        at(y, lax.rem(z + 2, SIDE), core) * bands + x,
        (frame - 2 * sign) * bands + x,
        at(lax.rem(y + 2, SIDE), z, core) * bands + x,
        (frame - 1 + 2 * core) * bands + x,
        (frame - 4 * sign) * bands + x,
    ]

    def pick(values, i):
        return sum((i == k).astype(jnp.int32) * values[k] for k in range(SLOTS))

    def attend(slot, h, initial):
        if initial:
            shift = jnp.float32(0)
        else:
            block = pick(block_of, slot)
            hits = sum(((kv_list[0, j] == block) & (j < kv_count[0])).astype(jnp.int32)
                       for j in range(kv_list.shape[1]))
            shift = jnp.where(hits > 0, jnp.float32(0), jnp.float32(UNLISTED))
        columns = pl.ds(pl.multiple_of(h * HEAD_DIM, HEAD_DIM), HEAD_DIM)
        key_rows = kv[slot, h, 0]
        value_rows = kv[slot, h, 1]
        count = key_rows.shape[0] // HEAD_DIM
        for r in range(0, q_ref.shape[0], ROWS):
            rows = pl.ds(r, ROWS)
            scores = lax.dot_general(q_ref[rows, columns], key_rows, (((1,), (1,)), ((), ())),
                                     preferred_element_type=jnp.float32)
            parts = [scores[:, i * HEAD_DIM:(i + 1) * HEAD_DIM] for i in range(count)]
            highest = functools.reduce(jnp.maximum, parts)
            highest = jnp.max(highest, axis=1, keepdims=True) * SCORE_SCALE + shift
            highest = jnp.broadcast_to(highest, (ROWS, HEAD_DIM))
            if not initial:
                before = top[rows, :]
                highest = jnp.maximum(before, highest)
            base = highest - shift
            weights = [jnp.exp2(p * SCORE_SCALE - base) for p in parts]
            added = functools.reduce(jnp.add, weights)
            rounded = jnp.concatenate([w.astype(jnp.bfloat16) for w in weights], axis=1)
            update = jnp.dot(rounded, value_rows, preferred_element_type=jnp.float32)
            top[rows, :] = highest
            if initial:
                sums[rows, :] = added
                acc[rows, :] = update
            else:
                rescale = jnp.exp2(before - highest)
                sums[rows, :] = sums[rows, :] * rescale + added
                acc[rows, :] = acc[rows, :] * rescale + update

    def attend_all(h):
        attend(OWN, h, True)

        def one(slot, carry):
            @pl.when(pick(valid, slot) > 0)
            def _():
                @pl.when((slot <= YLO) | (slot >= YOP))
                def _():
                    arrival(slot, h).wait_recv()

                attend(slot, h, False)

            return carry

        lax.fori_loop(1, SLOTS, one, 0)
        att[h, :, pl.ds(0, HEAD_DIM)] = (
            acc[...] / jnp.sum(sums[...], axis=1, keepdims=True)).astype(jnp.bfloat16)

    step = HEAD_DIM * 4

    def project(h, last):
        for c in range(0, width, step):
            columns = pl.ds(c, step)
            term = jnp.dot(att[h], wbuf[h, :, columns], preferred_element_type=jnp.float32)
            if last:
                out_ref[:, columns] = (total[:, columns] + term).astype(jnp.bfloat16)
            else:
                total[:, columns] += term

    pl.semaphore_wait(barrier, len(friends))

    for h in range(AHEAD):
        send_own(h)
        if h == 0:
            weight_piece(dev_head, 0, (1 - part) * width).start()
    total[...] = jnp.zeros_like(total)
    load_w.wait()

    def turn(t, carry):
        @pl.when(t + AHEAD < heads)
        def _():
            send_own(t + AHEAD)

        @pl.when(t < heads)
        def _():
            relay(t)

        @pl.when(t == 0)
        def _():
            weight_piece(dev_head, 0, (1 - part) * width).wait_recv()
            for k in (1, 2, 3):
                weight_relay(k).start()

        @pl.when(t == 2)
        def _():
            weight_cross().wait_recv()

        @pl.when(t >= 2)
        def _():
            copies(TO_HEAD, t - 2).wait_recv()
            project(t - 2, False)

        @pl.when(t >= 1)
        def _():
            h = t - 1
            relay_again(h)
            attend_all(h)
            copies(TO_HEAD, h).start()

        @pl.when(t == 1)
        def _():
            for k in (1, 2, 3):
                weight_relay(k).wait_recv()
            weight_cross().start()

        return carry

    lax.fori_loop(0, heads + 1, turn, 0)
    copies(TO_HEAD, heads - 1).wait_recv()
    project(heads - 1, True)

    def drain(h, carry):
        for kind in (TO_ZUP, TO_ZDOWN, RELAY_ZUP, RELAY_ZDOWN, TO_YDOWN, RELAY_YDOWN,
                     TO_CORE, TO_HEAD):
            copies(kind, h).wait_send()

        @pl.when(has_yup)
        def _():
            copies(TO_YUP, h).wait_send()
            copies(TO_EDGE2, h).wait_send()

        @pl.when(edge1_out)
        def _():
            copies(TO_EDGE1, h).wait_send()

        @pl.when(x > 0)
        def _():
            copies(TO_XDOWN, h).wait_send()

        @pl.when(x < SIDE - 1)
        def _():
            copies(TO_XUP, h).wait_send()

        @pl.when(gives_near)
        def _():
            near_copy(h, OWN).wait_send()

        return carry

    lax.fori_loop(0, heads, drain, 0)
    weight_piece(dev_head, 0, (1 - part) * width).wait_send()
    for k in (1, 2, 3):
        weight_relay(k).wait_send()
    weight_cross().wait_send()


def body(queries, keys, values, out_weight, kv_list, kv_count):
    tokens, features = queries.shape
    heads = features // HEAD_DIM
    model = out_weight.shape[1]
    weight = out_weight.reshape(heads, HEAD_DIM, model)
    vmem = pl.BlockSpec(memory_space=pltpu.VMEM)
    smem = pl.BlockSpec(memory_space=pltpu.SMEM)
    anywhere = pl.BlockSpec(memory_space=pl.ANY)
    return pl.pallas_call(
        functools.partial(kernel, heads),
        out_shape=jax.ShapeDtypeStruct((tokens, model // 2), jnp.bfloat16),
        in_specs=[smem, smem, vmem, anywhere, anywhere, anywhere],
        out_specs=vmem,
        scratch_shapes=[
            pltpu.VMEM((SLOTS, heads, 2, tokens, HEAD_DIM), jnp.bfloat16),
            pltpu.VMEM((heads, tokens, 2 * HEAD_DIM), jnp.bfloat16),
            pltpu.VMEM((heads, 2 * HEAD_DIM, model // 2), jnp.bfloat16),
            pltpu.VMEM((tokens, model // 2), jnp.float32),
            pltpu.VMEM((tokens, HEAD_DIM), jnp.float32),
            pltpu.VMEM((tokens, HEAD_DIM), jnp.float32),
            pltpu.VMEM((tokens, HEAD_DIM), jnp.float32),
            pltpu.SemaphoreType.DMA((SENDS, heads)),
            pltpu.SemaphoreType.DMA((SLOTS, heads)),
            pltpu.SemaphoreType.DMA((heads,)),
            pltpu.SemaphoreType.DMA((heads,)),
            pltpu.SemaphoreType.DMA((heads, 2)),
            pltpu.SemaphoreType.DMA,
            pltpu.SemaphoreType.DMA((SIDE + 1,)),
            pltpu.SemaphoreType.DMA((SIDE + 1,)),
        ],
        compiler_params=pltpu.CompilerParams(
            collective_id=0, has_side_effects=True, vmem_limit_bytes=56 * 1024 * 1024),
    )(kv_list, kv_count, queries, keys, values, weight)


def solution(mesh):
    rows = P(("tm", "height"), "head")
    return jax.shard_map(
        body,
        mesh=mesh,
        in_specs=(rows, rows, rows, P("head", None), P(("tm", "height"), None),
                  P(("tm", "height"))),
        out_specs=rows,
        check_vma=False,
    )
```

time: 478 us -> 202 us (0.42)
  waiting for transfers between devices: 260 us -> 0 us
  Pallas kernels: 0 us -> 198 us
  starting transfers between devices: 108 us -> 0 us
  local copies, waits for them, and re-layouts: 41.5 us -> 2.65 us
  matrix products: 22.6 us -> 0 us
  loops' own time: 16.6 us -> 0 us
  between operations: 13.6 us -> 0.66 us
  other arithmetic: 11.8 us -> 0 us
    pallas_call x0 -> x1, Pallas kernels: none -> 198 us  [body(): pl.pallas_call(functools.partial(kernel, heads), out_shape=jax.ShapeDtype...]
    reduce_scatter x1 -> x0, waiting for transfers between devices: 135 us -> none  [body(): lax.psum_scatter(partial_value.astype(jnp.bfloat16), 'head', scatter_dime...]
    ppermute x12 -> x0, waiting for transfers between devices: 125 us -> none  [the longest x2 80.8 us: extended(): lax.ppermute(lax.slice_in_dim(block, block.shape[dim] - width, None, axis...]
    ppermute x12 -> x0, starting transfers between devices: 108 us -> none  [the longest x8 93.3 us: passed_along(): lax.ppermute(value, axis, [(source, source + steps) for source in range(i...]
    unnamed x22 -> x1, local copies, waits for them, and re-layouts: 27.3 us -> 2.65 us
    dot_general x13 -> x0, matrix products: 22.6 us -> none  [the longest x6 10 us: attend_block(): jnp.einsum('hqk,khd->qhd', weights.astype(jnp.bfloat16), value_rows, pref...]
    another operation x1 -> x0, loops' own time: 16.6 us -> none  [body(): lax.fori_loop(0, listed_count, attend_block, (start_largest, start_totals...]
    slice x6 -> x0, local copies, waits for them, and re-layouts: 8.87 us -> none  [attend_block(): value_rows = chosen_pair[1].reshape(tokens_here, head_count, HEAD_DIM)]
  transfers between devices with their start and end apart: 13 -> 0, of which waited for: 5 -> 0; matrix products, arithmetic and copies ran while one was open for 5% -> 0% of each run, Pallas kernels for 0% -> 0%
where the time goes in v1:
time: 202 us; the launch traced here: 201 us
  Pallas kernels  198 us (98%)
  local copies, waits for them, and re-layouts  2.65 us (1%)
    pallas_call x1, Pallas kernels, body(): pl.pallas_call(functools.partial(kernel, heads), out_shape=jax.ShapeDtype...  198 us

profile of v1, /device:TPU:44, one launch (start us, length us, event | category | flops | bytes accessed | tf_op | source)
XLA Modules:
  0.0 201.4 jit_solution(11950676462064716246)
XLA Ops:
  0.7 198.1 %shard_map.64 = bf16[512,1536]{1,0:T(8,128)(2,1)} custom-call(s32[1,8]{1,0:T(1,128)} %kv_list.1, s32[1]{0:T(128)S(6)} %copy.8.kv_count, bf16[512,768]{1,0:T(8,128)(2,1)} %q_ref.1, bf16[512,768]{1,0:T(8,128)(2,1)} %k_hbm.1, bf16[512,768]{1,0:T(8,128)(2,1)} %v_hbm.1, bf16[6,128,3072]{2,1,0:T(8,128)(2,1)} %bitcast.1), custom_call_target="tpu_custom_call" | custom-call | tf_op jit(solution)/shard_map/pallas_call | solution.py:387
  198.8 2.7 %copy.9 = bf16[512,1536]{1,0:T(8,128)(2,1)} copy(bf16[512,1536]{1,0:T(8,128)(2,1)} %shard_map.64) | data formatting | bytes 3145728

commit v2 on v1

--- a/solution.py
+++ b/solution.py
@@ -11,8 +11,9 @@
 SIDE = 4
 SCORE_SCALE = HEAD_DIM ** (-0.5) * 1.4426950408889634
 UNLISTED = -1e30
-ROWS = 128
-AHEAD = 2
+ROWS = 512
+AHEAD = 1
+EARLY = 2
 
 OWN, OTHER, XLO, XHI, YLO, YHI, ZHI, ZLO, ZOP, EDGE1, YOP, NEAR, EDGE2 = range(13)
 SLOTS = 13
@@ -48,10 +49,11 @@
     dev_ydown = (at(ydown, z, core), x, part)
     dev_core = (at(y, z, 1 - core), x, part)
     dev_head = (tm, x, 1 - part)
+    dev_beside = (at(y, lax.rem(z + part + (1 - part) * 3, SIDE), core), x, 1 - part)
     dev_x = [None] + [(tm, lax.rem(x + k, SIDE), part) for k in (1, 2, 3)]
 
     barrier = pltpu.get_barrier_semaphore()
-    friends = [dev_zup, dev_zdown, dev_yup, dev_ydown, dev_core, dev_head] + dev_x[1:]
+    friends = [dev_zup, dev_zdown, dev_yup, dev_ydown, dev_core, dev_head, dev_beside] + dev_x[1:]
     for friend in friends:
         pl.semaphore_signal(barrier, inc=1, device_id=friend, device_id_type=pl.DeviceIdType.MESH)
 
@@ -294,7 +296,7 @@
     for h in range(AHEAD):
         send_own(h)
         if h == 0:
-            weight_piece(dev_head, 0, (1 - part) * width).start()
+            weight_piece(dev_beside, 0, (1 - part) * width).start()
     total[...] = jnp.zeros_like(total)
     load_w.wait()
 
@@ -307,9 +309,14 @@
         def _():
             relay(t)
 
+        @pl.when(t == heads - 1)
+        def _():
+            for early in range(EARLY):
+                copies(TO_HEAD, early).start()
+
         @pl.when(t == 0)
         def _():
-            weight_piece(dev_head, 0, (1 - part) * width).wait_recv()
+            weight_piece(dev_beside, 0, (1 - part) * width).wait_recv()
             for k in (1, 2, 3):
                 weight_relay(k).start()
 
@@ -317,17 +324,17 @@
         def _():
             weight_cross().wait_recv()
 
-        @pl.when(t >= 2)
-        def _():
-            copies(TO_HEAD, t - 2).wait_recv()
-            project(t - 2, False)
-
         @pl.when(t >= 1)
         def _():
             h = t - 1
             relay_again(h)
+
+            @pl.when(t == heads)
+            def _():
+                for early in range(EARLY, heads - 1):
+                    copies(TO_HEAD, early).start()
+
             attend_all(h)
-            copies(TO_HEAD, h).start()
 
         @pl.when(t == 1)
         def _():
@@ -338,6 +345,14 @@
         return carry
 
     lax.fori_loop(0, heads + 1, turn, 0)
+    copies(TO_HEAD, heads - 1).start()
+
+    def finish(h, carry):
+        copies(TO_HEAD, h).wait_recv()
+        project(h, False)
+        return carry
+
+    lax.fori_loop(0, heads - 1, finish, 0)
     copies(TO_HEAD, heads - 1).wait_recv()
     project(heads - 1, True)
 
@@ -370,7 +385,7 @@
         return carry
 
     lax.fori_loop(0, heads, drain, 0)
-    weight_piece(dev_head, 0, (1 - part) * width).wait_send()
+    weight_piece(dev_beside, 0, (1 - part) * width).wait_send()
     for k in (1, 2, 3):
         weight_relay(k).wait_send()
     weight_cross().wait_send()

time: 202 us -> 146 us (0.72); the launches traced: 201 us -> 143 us
  Pallas kernels: 198 us -> 140 us
    pallas_call x1, Pallas kernels: 198 us -> 140 us  [body(): pl.pallas_call(functools.partial(kernel, heads), out_shape=jax.ShapeDtype...]
where the time goes in v2:
time: 146 us; the launch traced here: 143 us
  Pallas kernels  140 us (96%)
  local copies, waits for them, and re-layouts  2.65 us (2%)
    pallas_call x1, Pallas kernels, body(): pl.pallas_call(functools.partial(kernel, heads), out_shape=jax.ShapeDtype...  140 us

profile of v2, /device:TPU:44, one launch (start us, length us, event | category | flops | bytes accessed | tf_op | source)
XLA Modules:
  0.0 143.3 jit_solution(9944816034440490937)
XLA Ops:
  0.7 140.0 %shard_map.64 = bf16[512,1536]{1,0:T(8,128)(2,1)} custom-call(s32[1,8]{1,0:T(1,128)} %kv_list.1, s32[1]{0:T(128)S(6)} %copy.8.kv_count, bf16[512,768]{1,0:T(8,128)(2,1)} %q_ref.1, bf16[512,768]{1,0:T(8,128)(2,1)} %k_hbm.1, bf16[512,768]{1,0:T(8,128)(2,1)} %v_hbm.1, bf16[6,128,3072]{2,1,0:T(8,128)(2,1)} %bitcast.1), custom_call_target="tpu_custom_call" | custom-call | tf_op jit(solution)/shard_map/pallas_call | solution.py:402
  140.7 2.7 %copy.9 = bf16[512,1536]{1,0:T(8,128)(2,1)} copy(bf16[512,1536]{1,0:T(8,128)(2,1)} %shard_map.64) | data formatting | bytes 3145728

commit v3 on v2

v3 whole, which is shorter than its diff:
```python
import functools

import jax
import jax.numpy as jnp
from jax import lax
from jax.experimental import pallas as pl
from jax.experimental.pallas import tpu as pltpu
from jax.sharding import PartitionSpec as P

HEAD_DIM = 128
SIDE = 4
SCORE_SCALE = HEAD_DIM ** (-0.5) * 1.4426950408889634
UNLISTED = -1e30
ROWS = 512
AGAIN, ATTEND = 1, 2

OWN, OTHER, XLO, XHI, YHI, ZP, ZM, ZOP, YOP, YLO, EDGE1, NEAR, EDGE2 = range(13)
LATE = YLO
SLOTS = 13
SOURCE = 13

(TO_ZP, TO_ZM, RELAY_Z, TO_MATE, MATE_Q, TO_YDOWN, RELAY_YDOWN, LAST_YDOWN, TO_YUP, TO_EDGE1,
 TO_EDGE2, TO_XDOWN, TO_XUP, TO_CORE, TO_NEAR, TO_HEAD) = range(16)
SENDS = 16


def kernel(heads, kv_list, kv_count, q_hbm, k_hbm, v_hbm, w_hbm, out_ref,
           kv, queries, att, wbuf, total, top, sums, acc,
           send, recv, recv_v, q_recv, att_recv, load, wload, wsend, wrecv):
    tm = lax.axis_index("tm")
    x = lax.axis_index("height")
    part = lax.axis_index("head")
    core = lax.rem(tm, 2)
    chip = lax.div(tm, 2)
    z = lax.rem(chip, SIDE)
    y = lax.div(chip, SIDE)
    far = lax.div(z, 2)
    sign = 1 - 2 * far
    ym = y * (1 - far) + (SIDE - 1 - y) * far
    zm = z * (1 - far) + (SIDE - 1 - z) * far

    def at(yy, zz, cc):
        return (yy * SIDE + zz) * 2 + cc

    swapped = 1 - lax.rem(z, 2)
    half = part * (1 - swapped) + (1 - part) * swapped
    ahead = 1 - 2 * half
    z_ahead = lax.rem(z + ahead + SIDE, SIDE)
    z_back = lax.rem(z - ahead + SIDE, SIDE)
    z_out = z_ahead * swapped + z_back * (1 - swapped)
    yup, ydown = lax.rem(y + sign + SIDE, SIDE), lax.rem(y - sign + SIDE, SIDE)
    dev_zp = (at(y, z_out, core), x, part * swapped + (1 - part) * (1 - swapped))
    dev_zm = (at(y, z_ahead, core), x, 1 - part)
    dev_relay = (at(y, z_out, core), x, 1 - part)
    dev_back = (at(y, z_back, core), x, 1 - part)
    dev_far = (at(y, z_ahead, core), x, part)
    dev_yup = (at(yup, z, core), x, part)
    dev_ydown = (at(ydown, z, core), x, part)
    dev_core = (at(y, z, 1 - core), x, part)
    dev_head = (tm, x, 1 - part)
    dev_beside = (at(y, lax.rem(z + part + (1 - part) * 3, SIDE), core), x, 1 - part)
    dev_x = [None] + [(tm, lax.rem(x + k, SIDE), part) for k in (1, 2, 3)]

    barrier = pltpu.get_barrier_semaphore()
    friends = [dev_zm, dev_back, dev_far, dev_yup, dev_ydown, dev_core, dev_head] + dev_x[1:]
    for friend in friends:
        pl.semaphore_signal(barrier, inc=1, device_id=friend, device_id_type=pl.DeviceIdType.MESH)

    source = OWN + (SOURCE - OWN) * swapped

    def columns_of(h):
        return pl.ds(pl.multiple_of(h * HEAD_DIM, HEAD_DIM), HEAD_DIM)

    def loads(h):
        return (pltpu.make_async_copy(k_hbm.at[:, columns_of(h)], kv.at[source, h, 0], load.at[h, 0]),
                pltpu.make_async_copy(v_hbm.at[:, columns_of(h)], kv.at[source, h, 1], load.at[h, 1]))

    def load_q(h):
        return pltpu.make_async_copy(q_hbm.at[:, columns_of(h)], queries.at[h], load.at[h, 2])

    for h in range(heads):
        for copy in loads(h):
            copy.start()

        @pl.when(swapped == 0)
        def _():
            load_q(h).start()

    width = w_hbm.shape[2] // 2

    def rows_of(heads_half):
        return pl.ds(pl.multiple_of(heads_half * HEAD_DIM, HEAD_DIM), HEAD_DIM)

    mine = pl.ds(pl.multiple_of(part * width, HEAD_DIM), width)
    load_w = pltpu.make_async_copy(w_hbm.at[:, :, mine], wbuf.at[:, rows_of(part), :], wload)
    load_w.start()

    has_yup = ym < SIDE - 1
    has_ydown = ym > 0
    edge1_out = (zm == 0) & has_yup
    edge1_in = (zm == 0) & has_ydown
    has_near = ((core == 0) & (chip > 0)) | ((core == 1) & (chip < SIDE * SIDE - 1))
    gives_near = ((core == 1) & (chip > 0)) | ((core == 0) & (chip < SIDE * SIDE - 1))
    near_at_edge = ((core == 1) & (z == 0)) | ((core == 0) & (z == SIDE - 1))
    half_is_first = 1 - half
    slot_after = ZM + (ZP - ZM) * half_is_first
    slot_before = ZP + (ZM - ZP) * half_is_first
    near_slot = slot_after * (1 - core) + slot_before * core
    edge_slot = slot_before * (1 - far) + slot_after * far
    relay_slot = ZP + (ZM - ZP) * swapped
    late_slot = ZM + (ZP - ZM) * swapped

    def remote(kind, h, src, dst, sem, device):
        return pltpu.make_async_remote_copy(
            src_ref=src, dst_ref=dst, send_sem=send.at[kind, h], recv_sem=sem,
            device_id=device, device_id_type=pl.DeviceIdType.MESH)

    def pair(kind, h, source, slot, device):
        return remote(kind, h, kv.at[source, h], kv.at[slot, h], recv.at[slot, h], device)

    def arrival(slot, h, device=None):
        return pair(TO_CORE, h, slot, slot, dev_core)

    def copies(kind, h):
        if kind == TO_ZP:
            return pair(kind, h, source, ZP, dev_zp)
        if kind == TO_ZM:
            return pair(kind, h, OWN, ZM, dev_zm)
        if kind == RELAY_Z:
            return pair(kind, h, relay_slot, ZOP, dev_relay)
        if kind == TO_MATE:
            return pair(kind, h, SOURCE, OWN, dev_head)
        if kind == MATE_Q:
            return remote(kind, h, q_hbm.at[:, columns_of(h)], queries.at[h], q_recv.at[h], dev_head)
        if kind == TO_YDOWN:
            return pair(kind, h, OWN, YHI, dev_ydown)
        if kind == RELAY_YDOWN:
            return pair(kind, h, YHI, YOP, dev_ydown)
        if kind == TO_YUP:
            return remote(kind, h, kv.at[OWN, h, 0], kv.at[YLO, h, 0], recv.at[YLO, h], dev_yup)
        if kind == LAST_YDOWN:
            return remote(kind, h, kv.at[YOP, h, 1], kv.at[YLO, h, 1], recv_v.at[h], dev_ydown)
        if kind == TO_EDGE1:
            return pair(kind, h, edge_slot, EDGE1, dev_yup)
        if kind == TO_EDGE2:
            return pair(kind, h, ZOP, EDGE2, dev_yup)
        if kind == TO_XDOWN:
            return pair(kind, h, OWN, XHI, dev_x[3])
        if kind == TO_XUP:
            return pair(kind, h, OWN, XLO, dev_x[1])
        if kind == TO_CORE:
            return pair(kind, h, OWN, OTHER, dev_core)
        if kind == TO_HEAD:
            piece = att.at[h, :, rows_of(half)]
            return remote(kind, h, piece, piece, att_recv.at[h], dev_head)

    def near_copy(h, slot):
        return pair(TO_NEAR, h, slot, NEAR, dev_core)

    def give(h):
        for copy in loads(h):
            copy.wait()

        @pl.when(swapped == 1)
        def _():
            copies(TO_MATE, h).start()

    def send_own(h):
        copies(TO_ZP, h).start()

        @pl.when(swapped == 1)
        def _():
            arrival(OWN, h).wait_recv()
            copies(MATE_Q, h).start()

        for kind in (TO_ZM, TO_YDOWN):
            copies(kind, h).start()

        @pl.when(has_yup)
        def _():
            copies(TO_YUP, h).start()

        @pl.when(x > 0)
        def _():
            copies(TO_XDOWN, h).start()

        @pl.when(x < SIDE - 1)
        def _():
            copies(TO_XUP, h).start()

        copies(TO_CORE, h).start()

    def relay(h):
        arrival(relay_slot, h).wait_recv()
        copies(RELAY_Z, h).start()
        arrival(YHI, h).wait_recv()
        copies(RELAY_YDOWN, h).start()

    def relay_again(h):
        arrival(late_slot, h).wait_recv()

        @pl.when(edge1_out)
        def _():
            copies(TO_EDGE1, h).start()

        @pl.when(gives_near & jnp.logical_not(near_at_edge))
        def _():
            near_copy(h, near_slot).start()

        arrival(YOP, h).wait_recv()

        @pl.when(ym != 1)
        def _():
            copies(LAST_YDOWN, h).start()

        arrival(ZOP, h).wait_recv()

        @pl.when(has_yup)
        def _():
            copies(TO_EDGE2, h).start()

    def relay_edge(h):
        @pl.when(has_ydown)
        def _():
            copies(TO_YUP, h).wait_recv()
            copies(LAST_YDOWN, h).wait_recv()

        @pl.when(edge1_in)
        def _():
            arrival(EDGE1, h).wait_recv()

        @pl.when(gives_near & near_at_edge)
        def _():
            near_copy(h, EDGE1).start()

    group = heads // 2
    chunk = width // SIDE

    def weight_piece():
        return pltpu.make_async_remote_copy(
            src_ref=w_hbm.at[pl.ds(core * group, group), :,
                             pl.ds(pl.multiple_of((1 - part) * width + x * chunk, HEAD_DIM), chunk)],
            dst_ref=wbuf.at[pl.ds(core * group, group), rows_of(part),
                            pl.ds(pl.multiple_of(x * chunk, HEAD_DIM), chunk)],
            send_sem=wsend.at[0], recv_sem=wrecv.at[0],
            device_id=dev_beside, device_id_type=pl.DeviceIdType.MESH)

    def weight_relay(k):
        piece = wbuf.at[pl.ds(core * group, group), rows_of(1 - part),
                        pl.ds(pl.multiple_of(x * chunk, HEAD_DIM), chunk)]
        return pltpu.make_async_remote_copy(
            src_ref=piece, dst_ref=piece, send_sem=wsend.at[k], recv_sem=wrecv.at[k],
            device_id=dev_x[k], device_id_type=pl.DeviceIdType.MESH)

    def weight_cross():
        piece = wbuf.at[pl.ds(core * group, group), rows_of(1 - part), :]
        return pltpu.make_async_remote_copy(
            src_ref=piece, dst_ref=piece, send_sem=wsend.at[SIDE], recv_sem=wrecv.at[SIDE],
            device_id=dev_core, device_id_type=pl.DeviceIdType.MESH)

    frame = tm
    bands = SIDE
    always = 1 + 0 * z
    valid = [always, always, x > 0, x < SIDE - 1, has_yup, (z + ahead >= 0) & (z + ahead < SIDE),
             (z - ahead >= 0) & (z - ahead < SIDE), always, always, has_ydown, edge1_in, has_near,
             has_ydown]
    valid = [jnp.int32(v) if isinstance(v, int) else v.astype(jnp.int32) for v in valid]
    block_of = [
        frame * bands + x,
        (frame + 1 - 2 * core) * bands + x,
        frame * bands + x - 1,
        frame * bands + x + 1,
        (frame + 8 * sign) * bands + x,
        (frame + 2 * ahead) * bands + x,
        (frame - 2 * ahead) * bands + x,
        at(y, lax.rem(z + 2, SIDE), core) * bands + x,
        at(lax.rem(y + 2, SIDE), z, core) * bands + x,
        (frame - 8 * sign) * bands + x,
        (frame - 2 * sign) * bands + x,
        (frame - 1 + 2 * core) * bands + x,
        (frame - 4 * sign) * bands + x,
    ]

    def pick(values, i):
        return sum((i == k).astype(jnp.int32) * values[k] for k in range(SLOTS))

    def attend(slot, h, initial):
        if initial:
            shift = jnp.float32(0)
        else:
            block = pick(block_of, slot)
            hits = sum(((kv_list[0, j] == block) & (j < kv_count[0])).astype(jnp.int32)
                       for j in range(kv_list.shape[1]))
            shift = jnp.where(hits > 0, jnp.float32(0), jnp.float32(UNLISTED))
        here = lax.rem(h, 2)
        key_rows = kv[slot, h, 0]
        value_rows = kv[slot, h, 1]
        count = key_rows.shape[0] // HEAD_DIM
        for r in range(0, queries.shape[1], ROWS):
            rows = pl.ds(r, ROWS)
            scores = lax.dot_general(queries[h, rows, :], key_rows, (((1,), (1,)), ((), ())),
                                     preferred_element_type=jnp.float32)
            parts = [scores[:, i * HEAD_DIM:(i + 1) * HEAD_DIM] for i in range(count)]
            highest = functools.reduce(jnp.maximum, parts)
            highest = jnp.max(highest, axis=1, keepdims=True) * SCORE_SCALE + shift
            highest = jnp.broadcast_to(highest, (ROWS, HEAD_DIM))
            if not initial:
                before = top[here, rows, :]
                highest = jnp.maximum(before, highest)
            base = highest - shift
            weights = [jnp.exp2(p * SCORE_SCALE - base) for p in parts]
            added = functools.reduce(jnp.add, weights)
            rounded = jnp.concatenate([w.astype(jnp.bfloat16) for w in weights], axis=1)
            update = jnp.dot(rounded, value_rows, preferred_element_type=jnp.float32)
            top[here, rows, :] = highest
            if initial:
                sums[here, rows, :] = added
                acc[here, rows, :] = update
            else:
                rescale = jnp.exp2(before - highest)
                sums[here, rows, :] = sums[here, rows, :] * rescale + added
                acc[here, rows, :] = acc[here, rows, :] * rescale + update

    def attend_slots(h, first, last):
        def one(slot, carry):
            @pl.when(pick(valid, slot) > 0)
            def _():
                @pl.when((slot <= XHI) | (slot >= NEAR))
                def _():
                    arrival(slot, h).wait_recv()

                attend(slot, h, False)

            return carry

        lax.fori_loop(first, last, one, 0)

    def attend_early(h):
        @pl.when(swapped == 1)
        def _():
            copies(MATE_Q, h).wait_recv()

        @pl.when(swapped == 0)
        def _():
            load_q(h).wait()

        attend(OWN, h, True)
        attend_slots(h, OTHER, LATE)

    def attend_late(h):
        attend_slots(h, LATE, SLOTS)
        here = lax.rem(h, 2)
        att[h, :, rows_of(half)] = (
            acc[here] / jnp.sum(sums[here], axis=1, keepdims=True)).astype(jnp.bfloat16)

    step = HEAD_DIM * 4

    def project(h, last):
        for c in range(0, width, step):
            columns = pl.ds(c, step)
            term = jnp.dot(att[h], wbuf[h, :, columns], preferred_element_type=jnp.float32)
            if last:
                out_ref[:, columns] = (total[:, columns] + term).astype(jnp.bfloat16)
            else:
                total[:, columns] += term

    pl.semaphore_wait(barrier, len(friends))

    give(0)
    send_own(0)
    give(1)
    total[...] = jnp.zeros_like(total)

    def turn(t, carry):
        @pl.when((t >= AGAIN) & (t < heads + AGAIN))
        def _():
            relay_again(t - AGAIN)

        @pl.when(t < heads)
        def _():
            relay(t)

        @pl.when(t + 1 < heads)
        def _():
            send_own(t + 1)

        @pl.when(t + 2 < heads)
        def _():
            give(t + 2)

        @pl.when(t == 1)
        def _():
            weight_piece().start()

        @pl.when(t == 3)
        def _():
            weight_piece().wait_recv()
            for k in (1, 2, 3):
                weight_relay(k).start()

        @pl.when(t == 5)
        def _():
            for k in (1, 2, 3):
                weight_relay(k).wait_recv()
            weight_cross().start()

        @pl.when(t >= ATTEND)
        def _():
            relay_edge(t - ATTEND)
            attend_late(t - ATTEND)
            copies(TO_HEAD, t - ATTEND).start()

        @pl.when((t >= 1) & (t <= heads))
        def _():
            attend_early(t - 1)

        return carry

    lax.fori_loop(0, heads + ATTEND, turn, 0)
    load_w.wait()
    weight_cross().wait_recv()

    def finish(h, carry):
        copies(TO_HEAD, h).wait_recv()
        project(h, False)
        return carry

    lax.fori_loop(0, heads - 1, finish, 0)
    copies(TO_HEAD, heads - 1).wait_recv()
    project(heads - 1, True)

    def drain(h, carry):
        for kind in (TO_ZP, TO_ZM, RELAY_Z, TO_YDOWN, RELAY_YDOWN, TO_CORE, TO_HEAD):
            copies(kind, h).wait_send()

        @pl.when(swapped == 1)
        def _():
            copies(TO_MATE, h).wait_send()
            copies(MATE_Q, h).wait_send()

        @pl.when(ym != 1)
        def _():
            copies(LAST_YDOWN, h).wait_send()

        @pl.when(has_yup)
        def _():
            copies(TO_YUP, h).wait_send()
            copies(TO_EDGE2, h).wait_send()

        @pl.when(edge1_out)
        def _():
            copies(TO_EDGE1, h).wait_send()

        @pl.when(x > 0)
        def _():
            copies(TO_XDOWN, h).wait_send()

        @pl.when(x < SIDE - 1)
        def _():
            copies(TO_XUP, h).wait_send()

        @pl.when(gives_near)
        def _():
            near_copy(h, OWN).wait_send()

        return carry

    lax.fori_loop(0, heads, drain, 0)
    weight_piece().wait_send()
    for k in (1, 2, 3):
        weight_relay(k).wait_send()
    weight_cross().wait_send()


def body(queries, keys, values, out_weight, kv_list, kv_count):
    tokens, features = queries.shape
    heads = features // HEAD_DIM
    model = out_weight.shape[1]
    weight = out_weight.reshape(heads, HEAD_DIM, model)
    vmem = pl.BlockSpec(memory_space=pltpu.VMEM)
    smem = pl.BlockSpec(memory_space=pltpu.SMEM)
    anywhere = pl.BlockSpec(memory_space=pl.ANY)
    return pl.pallas_call(
        functools.partial(kernel, heads),
        out_shape=jax.ShapeDtypeStruct((tokens, model // 2), jnp.bfloat16),
        in_specs=[smem, smem, anywhere, anywhere, anywhere, anywhere],
        out_specs=vmem,
        scratch_shapes=[
            pltpu.VMEM((SLOTS + 1, heads, 2, tokens, HEAD_DIM), jnp.bfloat16),
            pltpu.VMEM((heads, tokens, HEAD_DIM), jnp.bfloat16),
            pltpu.VMEM((heads, tokens, 2 * HEAD_DIM), jnp.bfloat16),
            pltpu.VMEM((heads, 2 * HEAD_DIM, model // 2), jnp.bfloat16),
            pltpu.VMEM((tokens, model // 2), jnp.float32),
            pltpu.VMEM((2, tokens, HEAD_DIM), jnp.float32),
            pltpu.VMEM((2, tokens, HEAD_DIM), jnp.float32),
            pltpu.VMEM((2, tokens, HEAD_DIM), jnp.float32),
            pltpu.SemaphoreType.DMA((SENDS, heads)),
            pltpu.SemaphoreType.DMA((SLOTS, heads)),
            pltpu.SemaphoreType.DMA((heads,)),
            pltpu.SemaphoreType.DMA((heads,)),
            pltpu.SemaphoreType.DMA((heads,)),
            pltpu.SemaphoreType.DMA((heads, 3)),
            pltpu.SemaphoreType.DMA,
            pltpu.SemaphoreType.DMA((SIDE + 1,)),
            pltpu.SemaphoreType.DMA((SIDE + 1,)),
        ],
        compiler_params=pltpu.CompilerParams(
            collective_id=0, has_side_effects=True, vmem_limit_bytes=56 * 1024 * 1024),
    )(kv_list, kv_count, queries, keys, values, weight)


def solution(mesh):
    rows = P(("tm", "height"), "head")
    return jax.shard_map(
        body,
        mesh=mesh,
        in_specs=(rows, rows, rows, P("head", None), P(("tm", "height"), None),
                  P(("tm", "height"))),
        out_specs=rows,
        check_vma=False,
    )
```

time: 146 us -> 143 us (0.979)
  the two profiles are of different devices: /device:TPU:44 before, /device:TPU:203 now
where the time goes in v3:
time: 143 us
  Pallas kernels  139 us (97%)
  local copies, waits for them, and re-layouts  2.65 us (2%)
    pallas_call x1, Pallas kernels, body(): pl.pallas_call(functools.partial(kernel, heads), out_shape=jax.ShapeDtype...  139 us

profile of v3, /device:TPU:203, one launch (start us, length us, event | category | flops | bytes accessed | tf_op | source)
XLA Modules:
  0.0 142.5 jit_solution(657655105926433191)
XLA Ops:
  0.7 139.2 %shard_map.64 = bf16[512,1536]{1,0:T(8,128)(2,1)} custom-call(s32[1,8]{1,0:T(1,128)} %kv_list.1, s32[1]{0:T(128)S(6)} %copy.8.kv_count, bf16[512,768]{1,0:T(8,128)(2,1)} %q_hbm.1, bf16[512,768]{1,0:T(8,128)(2,1)} %k_hbm.1, bf16[512,768]{1,0:T(8,128)(2,1)} %v_hbm.1, bf16[6,128,3072]{2,1,0:T(8,128)(2,1)} %bitcast.1), custom_call_target="tpu_custom_call" | custom-call | tf_op jit(solution)/shard_map/pallas_call | solution.py:483
  139.9 2.7 %copy.9 = bf16[512,1536]{1,0:T(8,128)(2,1)} copy(bf16[512,1536]{1,0:T(8,128)(2,1)} %shard_map.64) | data formatting | bytes 3145728

commit v4 on v3

--- a/solution.py
+++ b/solution.py
@@ -236,14 +236,14 @@
     group = heads // 2
     chunk = width // SIDE
 
-    def weight_piece():
+    def weight_piece(sem=0, device=dev_beside):
         return pltpu.make_async_remote_copy(
             src_ref=w_hbm.at[pl.ds(core * group, group), :,
                              pl.ds(pl.multiple_of((1 - part) * width + x * chunk, HEAD_DIM), chunk)],
             dst_ref=wbuf.at[pl.ds(core * group, group), rows_of(part),
                             pl.ds(pl.multiple_of(x * chunk, HEAD_DIM), chunk)],
-            send_sem=wsend.at[0], recv_sem=wrecv.at[0],
-            device_id=dev_beside, device_id_type=pl.DeviceIdType.MESH)
+            send_sem=wsend.at[sem], recv_sem=wrecv.at[0],
+            device_id=device, device_id_type=pl.DeviceIdType.MESH)
 
     def weight_relay(k):
         piece = wbuf.at[pl.ds(core * group, group), rows_of(1 - part),
@@ -390,7 +390,10 @@
 
         @pl.when(t == 1)
         def _():
-            weight_piece().start()
+            @pl.when(swapped == 0)
+            def _():
+                weight_piece().start()
+                weight_piece(SIDE + 1, dev_head).start()
 
         @pl.when(t == 3)
         def _():
@@ -466,7 +469,12 @@
         return carry
 
     lax.fori_loop(0, heads, drain, 0)
-    weight_piece().wait_send()
+
+    @pl.when(swapped == 0)
+    def _():
+        weight_piece().wait_send()
+        weight_piece(SIDE + 1, dev_head).wait_send()
+
     for k in (1, 2, 3):
         weight_relay(k).wait_send()
     weight_cross().wait_send()
@@ -501,8 +509,8 @@
             pltpu.SemaphoreType.DMA((heads,)),
             pltpu.SemaphoreType.DMA((heads, 3)),
             pltpu.SemaphoreType.DMA,
-            pltpu.SemaphoreType.DMA((SIDE + 1,)),
-            pltpu.SemaphoreType.DMA((SIDE + 1,)),
+            pltpu.SemaphoreType.DMA((SIDE + 2,)),
+            pltpu.SemaphoreType.DMA((SIDE + 2,)),
         ],
         compiler_params=pltpu.CompilerParams(
             collective_id=0, has_side_effects=True, vmem_limit_bytes=56 * 1024 * 1024),

time: 143 us -> 139 us (0.972)
  the two profiles are of different devices: /device:TPU:203 before, /device:TPU:44 now
where the time goes in v4:
time: 139 us
  Pallas kernels  136 us (98%)
  local copies, waits for them, and re-layouts  2.65 us (2%)
    pallas_call x1, Pallas kernels, body(): pl.pallas_call(functools.partial(kernel, heads), out_shape=jax.ShapeDtype...  136 us

profile of v4, /device:TPU:44, one launch (start us, length us, event | category | flops | bytes accessed | tf_op | source)
XLA Modules:
  0.0 138.8 jit_solution(6828713753249142867)
XLA Ops:
  0.7 135.5 %shard_map.64 = bf16[512,1536]{1,0:T(8,128)(2,1)} custom-call(s32[1,8]{1,0:T(1,128)} %kv_list.1, s32[1]{0:T(128)S(6)} %copy.8.kv_count, bf16[512,768]{1,0:T(8,128)(2,1)} %q_hbm.1, bf16[512,768]{1,0:T(8,128)(2,1)} %k_hbm.1, bf16[512,768]{1,0:T(8,128)(2,1)} %v_hbm.1, bf16[6,128,3072]{2,1,0:T(8,128)(2,1)} %bitcast.1), custom_call_target="tpu_custom_call" | custom-call | tf_op jit(solution)/shard_map/pallas_call | solution.py:491
  136.2 2.7 %copy.9 = bf16[512,1536]{1,0:T(8,128)(2,1)} copy(bf16[512,1536]{1,0:T(8,128)(2,1)} %shard_map.64) | data formatting | bytes 3145728

commit v5 on v4

--- a/solution.py
+++ b/solution.py
@@ -171,7 +171,6 @@
         @pl.when(swapped == 1)
         def _():
             arrival(OWN, h).wait_recv()
-            copies(MATE_Q, h).start()
 
         for kind in (TO_ZM, TO_YDOWN):
             copies(kind, h).start()
@@ -195,6 +194,10 @@
         copies(RELAY_Z, h).start()
         arrival(YHI, h).wait_recv()
         copies(RELAY_YDOWN, h).start()
+
+        @pl.when(swapped == 1)
+        def _():
+            copies(MATE_Q, h).start()
 
     def relay_again(h):
         arrival(late_slot, h).wait_recv()

time: 139 us -> 140 us (level); the launches traced: 139 us -> 138 us
  no operation moved by 1% of the time
where the time goes in v5:
time: 140 us; the launch traced here: 138 us
  Pallas kernels  135 us (96%)
  local copies, waits for them, and re-layouts  2.65 us (2%)
    pallas_call x1, Pallas kernels, body(): pl.pallas_call(functools.partial(kernel, heads), out_shape=jax.ShapeDtype...  135 us

profile of v5, /device:TPU:44, one launch (start us, length us, event | category | flops | bytes accessed | tf_op | source)
XLA Modules:
  0.0 138.0 jit_solution(53152902565402828)
XLA Ops:
  0.7 134.7 %shard_map.64 = bf16[512,1536]{1,0:T(8,128)(2,1)} custom-call(s32[1,8]{1,0:T(1,128)} %kv_list.1, s32[1]{0:T(128)S(6)} %copy.8.kv_count, bf16[512,768]{1,0:T(8,128)(2,1)} %q_hbm.1, bf16[512,768]{1,0:T(8,128)(2,1)} %k_hbm.1, bf16[512,768]{1,0:T(8,128)(2,1)} %v_hbm.1, bf16[6,128,3072]{2,1,0:T(8,128)(2,1)} %bitcast.1), custom_call_target="tpu_custom_call" | custom-call | tf_op jit(solution)/shard_map/pallas_call | solution.py:494
  135.4 2.7 %copy.9 = bf16[512,1536]{1,0:T(8,128)(2,1)} copy(bf16[512,1536]{1,0:T(8,128)(2,1)} %shard_map.64) | data formatting | bytes 3145728
